TPU v7x, 32 devices: a whole 2x2x4 slice. The times are simulated.
32 devices in a mesh: groups: 2 (over y), shard: 4 (over z), sub: 4 (over x, core).
Axes of the slice: x: 2, y: 2, z: 4, core: 2. Of those that a mesh axis runs over, the one named last changes fastest.
Arguments:
- queries: bfloat16 [512, 32, 128], P(('groups', 'shard', 'sub')), parts along dimension 0, may hold values from -6 to 6
- passages: bfloat16 [8192, 64, 128], P(('groups', 'shard', 'sub')), parts along dimension 0, may hold values from -0.5 to 0.5
- pass_len: int32 [8192], P(('groups', 'shard', 'sub')), parts along dimension 0, may hold values from 1 to 64
- owners: int32 [512, 8], P(('groups', 'shard', 'sub')), parts along dimension 0, may hold values from 0 to 15, all different within a row; in each aligned block of 16 rows (0 to 15, 16 to 31, ...) at most 16 rows name the same one
- candidates: int32 [512, 8, 16], P(('groups', 'shard', 'sub')), parts along dimension 0, may hold values from 0 to 255
Outputs:
- scores: float32 [512, 8, 16], P(('groups', 'shard', 'sub')), parts along dimension 0
There are 2 independent parts, one for each index of `groups`. A program takes and returns all parts, laid end to end along the dimension named above; each array names one. Nothing has to cross between parts.
Inputs may be any that keep to these rules, and one draw needn't show every extreme that they name: Each query's 8 owners are distinct; among the 16 queries of one device no owner is named more than 16 times, a bound that some block reaches.
All inputs are finite; a program needn't handle non-finite values.
Results may differ from a plain program's by a relative error of at most 0.0003.
Values may be sent and summed in bfloat16 or wider, within the bound.
A program may use at most 64 MiB of HBM per device.

v0:
```python
import jax
import jax.numpy as jnp
from jax import lax
from jax.experimental import pallas as pl
from jax.experimental.pallas import tpu as pltpu
from jax.sharding import PartitionSpec as P

AXES = ("shard", "sub")


def score_kernel(route_ref, cand_ref, q_ref, passages_ref, out_ref, maxima, live):
    slots, query_len, feature = q_ref.shape
    tokens = passages_ref.shape[1]
    cand_count = out_ref.shape[1]
    groups = cand_count // 2
    maxima[...] = jnp.zeros_like(maxima)

    def collect(slot, count):
        live[count] = slot
        return count + (route_ref[0, 0, slot] >= 0).astype(jnp.int32)

    count = lax.fori_loop(0, slots, collect, jnp.int32(0), unroll=8)
    live[count] = live[jnp.maximum(count - 1, 0)]
    blank = jnp.zeros((query_len, feature), jnp.bfloat16)

    def one(slot):
        base = route_ref[0, 0, slot] * cand_count
        tok = q_ref[slot]
        weights = jnp.concatenate(
            [jnp.concatenate([tok, blank], 1), jnp.concatenate([blank, tok], 1)], 0
        )
        rows = [passages_ref[cand_ref[slot, base + k]] for k in range(cand_count)]
        left = jnp.concatenate(rows[:groups], 0)
        right = jnp.concatenate(rows[groups:], 0)
        similar = lax.dot_general(
            jnp.concatenate([left, right], 1),
            weights,
            (((1,), (1,)), ((), ())),
            preferred_element_type=jnp.float32,
        )
        for g in range(groups):
            best = jnp.max(similar[g * tokens : (g + 1) * tokens], axis=0, keepdims=True)
            maxima[g, pl.ds(slot, 1), :] = best

    def pair(step, carry):
        one(live[2 * step])
        one(live[2 * step + 1])
        return carry

    lax.fori_loop(0, (count + 1) // 2, pair, 0)

    width = 2 * query_len
    lane = lax.broadcasted_iota(jnp.int32, (width, cand_count), 0)
    column = lax.broadcasted_iota(jnp.int32, (width, cand_count), 1)
    total = jnp.zeros((slots, cand_count), jnp.float32)
    for g in range(groups):
        pick = column == g + groups * (lane >= query_len).astype(jnp.int32)
        pick = pick.astype(jnp.float32).astype(jnp.bfloat16)
        value = maxima[g]
        for _ in range(3):
            part = value.astype(jnp.bfloat16)
            total = total + jnp.dot(part, pick, preferred_element_type=jnp.float32)
            value = value - part.astype(jnp.float32)
    out_ref[...] = total * (1.0 / query_len)


def score_slots(route, cand, queries, passages):
    slots, query_len, feature = queries.shape
    cand_count = 16
    block = min(slots, 256)
    return pl.pallas_call(
        score_kernel,
        grid=(slots // block,),
        out_shape=jax.ShapeDtypeStruct((slots, cand_count), jnp.float32),
        in_specs=[
            pl.BlockSpec((1, 1, block), lambda i: (i, 0, 0), memory_space=pltpu.SMEM),
            pl.BlockSpec((block, cand.shape[1]), lambda i: (i, 0), memory_space=pltpu.SMEM),
            pl.BlockSpec((block, query_len, feature), lambda i: (i, 0, 0)),
            pl.BlockSpec(passages.shape, lambda i: (0, 0, 0)),
        ],
        out_specs=pl.BlockSpec((block, cand_count), lambda i: (i, 0)),
        scratch_shapes=[
            pltpu.VMEM((cand_count // 2, block, 2 * query_len), jnp.float32),
            pltpu.SMEM((block + 1,), jnp.int32),
        ],
        compiler_params=pltpu.CompilerParams(vmem_limit_bytes=48 << 20),
    )(route.reshape(slots // block, 1, block), cand, queries, passages)


def body(queries, passages, pass_len, owners, candidates):
    owner_count = lax.axis_size("shard") * lax.axis_size("sub")
    me = lax.axis_index(AXES)
    query_count, route_count, cand_count = candidates.shape
    tokens = passages.shape[1]
    slot_pos = lax.broadcasted_iota(jnp.int32, (1, tokens, 1), 1)
    filled = jnp.where(slot_pos < pass_len[:, None, None], passages, passages[:, :1, :])
    all_q = lax.all_gather(queries, AXES, axis=0, tiled=True)
    flat = candidates.reshape(query_count, route_count * cand_count)
    packed = jnp.concatenate([flat, jnp.pad(owners, ((0, 0), (0, 128 - route_count)), constant_values=-1)], axis=1)
    all_ids = lax.all_gather(packed, AXES, axis=0, tiled=True)
    all_cand = all_ids[:, : route_count * cand_count]
    all_owners = all_ids[:, route_count * cand_count : route_count * cand_count + route_count]
    numbers = jnp.arange(1, route_count + 1, dtype=jnp.int32)
    route = jnp.sum(jnp.where(all_owners == me, numbers[None, :], 0), axis=1) - 1
    owned = score_slots(route, all_cand, all_q, filled)
    returned = lax.all_to_all(
        owned.reshape(owner_count, query_count, cand_count), AXES, split_axis=0, concat_axis=0, tiled=True
    )
    hit = owners[None, :, :] == jnp.arange(owner_count, dtype=jnp.int32)[:, None, None]
    return jnp.sum(jnp.where(hit[..., None], returned[:, :, None, :], 0.0), axis=0)


def solution(mesh):
    in_specs = (
        P(("groups", "shard", "sub"), None, None),
        P(("groups", "shard", "sub"), None, None),
        P(("groups", "shard", "sub")),
        P(("groups", "shard", "sub"), None),
        P(("groups", "shard", "sub"), None, None),
    )
    out_specs = P(("groups", "shard", "sub"), None, None)
    return jax.shard_map(body, mesh=mesh, in_specs=in_specs, out_specs=out_specs, check_vma=False)
```

profile of v0, /device:TPU:0, one launch (start us, length us, event | category | flops | bytes accessed | tf_op | source)
XLA Modules:
  0.0 116.9 jit_solution(11185635692538084851)
XLA Ops:
  6.5 0.0 all-gather.2.cloned.1.call-start
  6.5 0.7 all-gather.2.cloned.1.call-update
  7.3 0.8 copy.14
  8.0 0.9 reshape.50
  9.0 24.1 %all_gather.6 = s32[256,256]{1,0:T(8,128)S(1)} all-gather(s32[16,256]{1,0:T(8,128)S(1)} %select_add_fusion), channel_id=1, replica_groups=mesh['groups'=2,'shard'=4,'sub'=4] {'shard','sub'}, dimensions={0}, use_global_device_ids=true | all-gather | bytes 278528 | tf_op jit(solution)/shard_map/all_gather | solution.py:100
  33.1 1.1 slice.11
  34.2 0.1 select_reduce_fusion.1
  34.3 0.8 iota_compare_fusion
  35.1 7.8 %broadcast_select_fusion.passages_ref = bf16[256,64,128]{2,1,0:T(8,128)(2,1)} fusion(bf16[256,64,128]{2,1,0:T(8,128)(2,1)} %param.6, pred[256,64]{1,0:T(8,128)(4,1)S(1)} %iota_compare_fusion, bf16[256,128]{1,0:T(8,128)(2,1)S(1)} %bitcast.7), kind=kLoop, calls=%fused_computation | loop fusion | flops 2097152 | bytes 8470528 | tf_op jit(solution)/shard_map/jit(_where)/select_n | solution.py:96
  43.0 10.9 %all-gather.2.cloned.1.call-done.q_ref = bf16[256,32,128]{2,1,0:T(8,128)(2,1)} async-done(((bf16[16,32,128]{2,1,0:T(8,128)(2,1)}), bf16[256,32,128]{2,1,0:T(8,128)(2,1)}) %all-gather.2.cloned.1.call-update) | async-done | bytes 2097168 | tf_op jit(solution)/shard_map/all_gather | solution.py:97
  53.8 0.0 copy-start
  53.8 1.6 %copy-done = bf16[256,32,128]{2,1,0:T(8,128)(2,1)S(1)} copy-done((bf16[256,32,128]{2,1,0:T(8,128)(2,1)S(1)}, bf16[256,32,128]{2,1,0:T(8,128)(2,1)}, u32[]{:S(2)}) %copy-start) | copy-done | bytes 2097176
  55.4 27.3 %shard_map.55 = f32[256,16]{1,0:T(8,128)S(1)} custom-call(s32[1,1,256]{2,1,0:T(1,128)S(1)} %bitcast.6, s32[256,128]{1,0:T(8,128)S(1)} %slice.13.cand_ref, bf16[256,32,128]{2,1,0:T(8,128)(2,1)S(1)} %copy-done, bf16[256,64,128]{2,1,0:T(8,128)(2,1)} %broadcast_select_fusion.passages_ref), custom_call_target="tpu_custom_call" | custom-call | tf_op jit(solution)/shard_map/pallas_call | solution.py:71
  82.7 0.7 reshape.52
  83.4 17.9 %all-to-all-start = ((f32[16,1,256]{2,1,0:T(1,128)}), f32[16,1,256]{2,1,0:T(1,128)S(1)}, u32[]{:S(2)}, u32[]{:S(2)}) async-start(f32[16,1,256]{2,1,0:T(1,128)} %reshape.52), calls=%async_computation | async-start | bytes 32768 | tf_op jit(solution)/shard_map/all_to_all | solution.py:106
  101.3 6.5 %all-to-all-done = f32[16,1,256]{2,1,0:T(1,128)S(1)} async-done(((f32[16,1,256]{2,1,0:T(1,128)}), f32[16,1,256]{2,1,0:T(1,128)S(1)}, u32[]{:S(2)}, u32[]{:S(2)}) %all-to-all-start) | async-done | bytes 16416 | tf_op jit(solution)/shard_map/all_to_all | solution.py:106
  107.8 0.5 broadcast.54
  108.3 0.7 reduce
  109.0 0.1 reshape.53
  109.1 1.0 select_reduce_fusion
  (6 shorter events, 0.1 us)
Async XLA Ops:
  6.5 47.3 %all-gather.2.cloned.1.call-start = ((), (), s32[]{:S(2)}) async-start(), calls=%async_computation.1 | async-start | bytes 2228224 | tf_op jit(solution)/shard_map/all_gather | solution.py:97
  53.8 1.6 %copy-start = (bf16[256,32,128]{2,1,0:T(8,128)(2,1)S(1)}, bf16[256,32,128]{2,1,0:T(8,128)(2,1)}, u32[]{:S(2)}) copy-start(bf16[256,32,128]{2,1,0:T(8,128)(2,1)} %all-gather.2.cloned.1.call-done.q_ref) | copy-start | bytes 6291460
  83.4 24.4 %all-to-all-start = ((f32[16,1,256]{2,1,0:T(1,128)}), f32[16,1,256]{2,1,0:T(1,128)S(1)}, u32[]{:S(2)}, u32[]{:S(2)}) async-start(f32[16,1,256]{2,1,0:T(1,128)} %reshape.52), calls=%async_computation | async-start | bytes 32768 | tf_op jit(solution)/shard_map/all_to_all | solution.py:106
Sparse Core Ops, SparseCore 0:
  9.5 44.2 all-gather.1
where the time goes:
time: 117 us
  Pallas kernels  27.3 us (23%)
  blocking collectives  24.1 us (21%)
  waiting for transfers between devices  18 us (15%)
  starting transfers between devices  17.9 us (15%)
  between operations  13.5 us (12%)
  other arithmetic  10.4 us (9%)
  local copies, waits for them, and re-layouts  5.72 us (5%)
    pallas_call x1, Pallas kernels, score_slots(): pl.pallas_call(score_kernel, grid=(slots // block,), out_shape=jax.ShapeD...  27.3 us
    all_gather x1, blocking collectives, body(): all_ids = lax.all_gather(packed, AXES, axis=0, tiled=True)  24.1 us
    all_to_all x1, starting transfers between devices, body(): lax.all_to_all(owned.reshape(owner_count, query_count, cand_count), AXES,...  17.9 us
    all_gather x1, waiting for transfers between devices, body(): all_q = lax.all_gather(queries, AXES, axis=0, tiled=True)  10.9 us
    select_n x1, other arithmetic, body(): jnp.where(slot_pos < pass_len[:, None, None], passages, passages[:, :1, :])  7.82 us
    all_to_all x1, waiting for transfers between devices, body(): lax.all_to_all(owned.reshape(owner_count, query_count, cand_count), AXES,...  6.47 us
    unnamed x6, local copies, waits for them, and re-layouts  3.17 us
  transfers between devices with their start and end apart: 2, of which 2 were waited for; matrix products, arithmetic and copies ran while one was open for 10% of the time, Pallas kernels for 0%

commit v1 on v0

v1 whole, which is shorter than its diff:
```python
import jax
import jax.numpy as jnp
from jax import lax
from jax.experimental import pallas as pl
from jax.experimental.pallas import tpu as pltpu
from jax.sharding import PartitionSpec as P

def place(peer):
    subs = lax.axis_size("sub")
    return {"shard": peer // subs, "sub": lax.rem(peer, subs)}


def greet(me, count):
    barrier = pltpu.get_barrier_semaphore()

    def signal(off, carry):
        peer = lax.rem(me + off, count)
        pl.semaphore_signal(barrier, inc=1, device_id=place(peer), device_id_type=pl.DeviceIdType.MESH)
        return carry

    lax.fori_loop(1, count, signal, 0)
    pl.semaphore_wait(barrier, count - 1)


def position():
    return lax.axis_index("shard") * lax.axis_size("sub") + lax.axis_index("sub")


def gather_kernel(q_ref, ids_ref, all_q, all_ids, own_sem, q_send, q_recv, ids_send, ids_recv):
    count = ids_ref.shape[0]
    me = position()
    local_q = pltpu.make_async_copy(q_ref, all_q.at[me], own_sem.at[0])
    local_ids = pltpu.make_async_copy(ids_ref.at[me], all_ids.at[me], own_sem.at[1])
    local_q.start()
    local_ids.start()
    greet(me, count)

    def copies(off):
        peer = lax.rem(me + off, count)
        ids = pltpu.make_async_remote_copy(
            src_ref=ids_ref.at[peer],
            dst_ref=all_ids.at[me],
            send_sem=ids_send.at[off],
            recv_sem=ids_recv.at[off],
            device_id=place(peer),
            device_id_type=pl.DeviceIdType.MESH,
        )
        tok = pltpu.make_async_remote_copy(
            src_ref=q_ref,
            dst_ref=all_q.at[me],
            send_sem=q_send.at[off],
            recv_sem=q_recv.at[off],
            device_id=place(peer),
            device_id_type=pl.DeviceIdType.MESH,
        )
        return ids, tok

    def start(off, carry):
        ids, tok = copies(off)
        ids.start()
        tok.start()
        return carry

    def finish(off, carry):
        ids, tok = copies(off)
        ids.wait()
        tok.wait()
        return carry

    lax.fori_loop(1, count, start, 0)
    lax.fori_loop(1, count, finish, 0)
    local_q.wait()
    local_ids.wait()


def gather(queries, ids):
    count = ids.shape[0]
    return pl.pallas_call(
        gather_kernel,
        out_shape=(
            jax.ShapeDtypeStruct((count,) + queries.shape, queries.dtype),
            jax.ShapeDtypeStruct(ids.shape, ids.dtype),
        ),
        in_specs=[pl.BlockSpec(memory_space=pl.ANY)] * 2,
        out_specs=[pl.BlockSpec(memory_space=pl.ANY)] * 2,
        scratch_shapes=[pltpu.SemaphoreType.DMA((2,))] + [pltpu.SemaphoreType.DMA((count,))] * 4,
        compiler_params=pltpu.CompilerParams(collective_id=0, has_side_effects=True),
    )(queries, ids)


def return_kernel(owned_ref, out_ref, own_sem, send, recv):
    count = owned_ref.shape[0]
    me = position()
    local = pltpu.make_async_copy(owned_ref.at[me], out_ref.at[me], own_sem)
    local.start()
    greet(me, count)

    def copy(off):
        peer = lax.rem(me + off, count)
        return pltpu.make_async_remote_copy(
            src_ref=owned_ref.at[peer],
            dst_ref=out_ref.at[me],
            send_sem=send.at[off],
            recv_sem=recv.at[off],
            device_id=place(peer),
            device_id_type=pl.DeviceIdType.MESH,
        )

    def start(off, carry):
        copy(off).start()
        return carry

    def finish(off, carry):
        copy(off).wait()
        return carry

    lax.fori_loop(1, count, start, 0)
    lax.fori_loop(1, count, finish, 0)
    local.wait()


def give_back(owned):
    count = owned.shape[0]
    return pl.pallas_call(
        return_kernel,
        out_shape=jax.ShapeDtypeStruct(owned.shape, owned.dtype),
        in_specs=[pl.BlockSpec(memory_space=pl.ANY)],
        out_specs=pl.BlockSpec(memory_space=pl.ANY),
        scratch_shapes=[pltpu.SemaphoreType.DMA] + [pltpu.SemaphoreType.DMA((count,))] * 2,
        compiler_params=pltpu.CompilerParams(collective_id=1, has_side_effects=True),
    )(owned)


def score_kernel(ids_ref, len_ref, q_ref, passages_ref, out_ref, maxima, filled, live):
    sources, per_source, query_len, feature = q_ref.shape
    slots = sources * per_source
    passage_count, tokens, _ = passages_ref.shape
    cand_count = out_ref.shape[-1]
    groups = cand_count // 2
    maxima[...] = jnp.zeros_like(maxima)

    @pl.when(pl.program_id(0) == 0)
    def _():
        slot_pos = lax.broadcasted_iota(jnp.int32, (tokens, feature), 0)

        def fill(p, carry):
            values = passages_ref[p].astype(jnp.float32)
            values = jnp.where(slot_pos < len_ref[p], values, values[0:1])
            filled[p] = values.astype(jnp.bfloat16)
            return carry

        lax.fori_loop(0, passage_count, fill, 0, unroll=8)

    count = jnp.int32(0)
    for query in range(per_source):

        def collect(source, count, query=query):
            live[count] = source * per_source + query
            return count + (ids_ref[source, per_source, query] >= 0).astype(jnp.int32)

        count = lax.fori_loop(0, sources, collect, count, unroll=True)
    live[count] = live[jnp.maximum(count - 1, 0)]
    blank = jnp.zeros((query_len, feature), jnp.bfloat16)

    def one(slot):
        source, query = slot // per_source, lax.rem(slot, per_source)
        base = ids_ref[source, per_source, query] * cand_count
        tok = q_ref[source, query]
        weights = jnp.concatenate(
            [jnp.concatenate([tok, blank], 1), jnp.concatenate([blank, tok], 1)], 0
        )
        rows = [filled[ids_ref[source, query, base + k]] for k in range(cand_count)]
        left = jnp.concatenate(rows[:groups], 0)
        right = jnp.concatenate(rows[groups:], 0)
        similar = lax.dot_general(
            jnp.concatenate([left, right], 1),
            weights,
            (((1,), (1,)), ((), ())),
            preferred_element_type=jnp.float32,
        )
        for g in range(groups):
            best = jnp.max(similar[g * tokens : (g + 1) * tokens], axis=0, keepdims=True)
            maxima[g, pl.ds(slot, 1), :] = best

    def pair(step, carry):
        one(live[2 * step])
        one(live[2 * step + 1])
        return carry

    lax.fori_loop(0, (count + 1) // 2, pair, 0)

    width = 2 * query_len
    lane = lax.broadcasted_iota(jnp.int32, (width, cand_count), 0)
    column = lax.broadcasted_iota(jnp.int32, (width, cand_count), 1)
    total = jnp.zeros((slots, cand_count), jnp.float32)
    for g in range(groups):
        pick = column == g + groups * (lane >= query_len).astype(jnp.int32)
        pick = pick.astype(jnp.float32).astype(jnp.bfloat16)
        value = maxima[g]
        for _ in range(3):
            part = value.astype(jnp.bfloat16)
            total = total + jnp.dot(part, pick, preferred_element_type=jnp.float32)
            value = value - part.astype(jnp.float32)
    out_ref[...] = (total * (1.0 / query_len)).reshape(out_ref.shape)


def score_slots(ids, pass_len, queries, passages, cand_count):
    count, per_source, query_len, feature = queries.shape
    sources = min(count, 16)
    slots = sources * per_source
    return pl.pallas_call(
        score_kernel,
        grid=(count // sources,),
        out_shape=jax.ShapeDtypeStruct((count, per_source, cand_count), jnp.float32),
        in_specs=[
            pl.BlockSpec((sources,) + ids.shape[1:], lambda i: (i, 0, 0), memory_space=pltpu.SMEM),
            pl.BlockSpec(memory_space=pltpu.SMEM),
            pl.BlockSpec((sources, per_source, query_len, feature), lambda i: (i, 0, 0, 0)),
            pl.BlockSpec(passages.shape, lambda i: (0, 0, 0)),
        ],
        out_specs=pl.BlockSpec((sources, per_source, cand_count), lambda i: (i, 0, 0)),
        scratch_shapes=[
            pltpu.VMEM((cand_count // 2, slots, 2 * query_len), jnp.float32),
            pltpu.VMEM(passages.shape, passages.dtype),
            pltpu.SMEM((slots + 1,), jnp.int32),
        ],
        compiler_params=pltpu.CompilerParams(vmem_limit_bytes=48 << 20),
    )(ids, pass_len, queries, passages)


def body(queries, passages, pass_len, owners, candidates):
    owner_count = lax.axis_size("shard") * lax.axis_size("sub")
    query_count, route_count, cand_count = candidates.shape
    flat = candidates.reshape(query_count, route_count * cand_count)
    owner_ids = jnp.arange(owner_count, dtype=jnp.int32)
    numbers = jnp.arange(1, route_count + 1, dtype=jnp.int32)
    hit = owners[None, :, :] == owner_ids[:, None, None]
    route = jnp.sum(jnp.where(hit, numbers, 0), axis=2) - 1
    route = jnp.pad(route[:, None, :], ((0, 0), (0, 7), (0, flat.shape[1] - query_count)))
    ids = jnp.concatenate([jnp.broadcast_to(flat[None], (owner_count,) + flat.shape), route], axis=1)
    all_q, all_ids = gather(queries, ids)
    returned = give_back(score_slots(all_ids, pass_len, all_q, passages, cand_count))
    return jnp.sum(jnp.where(hit[..., None], returned[:, :, None, :], 0.0), axis=0)


def solution(mesh):
    in_specs = (
        P(("groups", "shard", "sub"), None, None),
        P(("groups", "shard", "sub"), None, None),
        P(("groups", "shard", "sub")),
        P(("groups", "shard", "sub"), None),
        P(("groups", "shard", "sub"), None, None),
    )
    out_specs = P(("groups", "shard", "sub"), None, None)
    return jax.shard_map(body, mesh=mesh, in_specs=in_specs, out_specs=out_specs, check_vma=False)
```

time: 117 us -> 115 us (0.983)
  Pallas kernels: 27.3 us -> 108 us
  blocking collectives: 24.1 us -> 0 us
  waiting for transfers between devices: 18 us -> 0 us
  starting transfers between devices: 17.9 us -> 0 us
  between operations: 13.5 us -> 0.1 us
  other arithmetic: 10.4 us -> 3.4 us
    pallas_call x1 -> x3, Pallas kernels: 27.3 us -> 108 us  [the longest x1 48.9 us: give_back(): pl.pallas_call(return_kernel, out_shape=jax.ShapeDtypeStruct(owned.shape,...]
    all_gather x1 -> x0, blocking collectives: 24.1 us -> none  [body(): all_ids = lax.all_gather(packed, AXES, axis=0, tiled=True)]
    all_to_all x1 -> x0, starting transfers between devices: 17.9 us -> none  [body(): lax.all_to_all(owned.reshape(owner_count, query_count, cand_count), AXES,...]
    all_gather x1 -> x0, waiting for transfers between devices: 10.9 us -> none  [body(): all_q = lax.all_gather(queries, AXES, axis=0, tiled=True)]
    select_n x1 -> x0, other arithmetic: 7.82 us -> none  [body(): jnp.where(slot_pos < pass_len[:, None, None], passages, passages[:, :1, :])]
    all_to_all x1 -> x0, waiting for transfers between devices: 6.47 us -> none  [body(): lax.all_to_all(owned.reshape(owner_count, query_count, cand_count), AXES,...]
    unnamed x6 -> x10, local copies, waits for them, and re-layouts: 3.17 us -> 3.84 us
  transfers between devices with their start and end apart: 2 -> 0, of which waited for: 2 -> 0; matrix products, arithmetic and copies ran while one was open for 10% -> 0% of each run, Pallas kernels for 0% -> 0%
where the time goes in v1:
time: 115 us; the launch traced here: 116 us
  Pallas kernels  108 us (94%)
  local copies, waits for them, and re-layouts  4.9 us (4%)
  other arithmetic  3.4 us (3%)
    pallas_call x1, Pallas kernels, give_back(): pl.pallas_call(return_kernel, out_shape=jax.ShapeDtypeStruct(owned.shape,...  48.9 us
    pallas_call x1, Pallas kernels, gather(): pl.pallas_call(gather_kernel, out_shape=(jax.ShapeDtypeStruct((count,) +...  44.3 us
    pallas_call x1, Pallas kernels, score_slots(): pl.pallas_call(score_kernel, grid=(count // sources,), out_shape=jax.Shap...  14.3 us
    unnamed x10, local copies, waits for them, and re-layouts  3.84 us

profile of v1, /device:TPU:0, one launch (start us, length us, event | category | flops | bytes accessed | tf_op | source)
XLA Modules:
  0.0 115.9 jit_solution(8820259938128420252)
XLA Ops:
  0.0 0.0 copy-start.4
  0.0 0.9 broadcast_in_dim.41
  1.0 0.8 select_reduce_fusion.1
  1.8 0.7 pad_add_fusion.ids_ref
  2.5 44.3 %shard_map.55 = (bf16[16,16,32,128]{3,2,1,0:T(8,128)(2,1)}, s32[16,24,128]{2,1,0:T(8,128)}) custom-call(bf16[16,32,128]{2,1,0:T(8,128)(2,1)} %q_ref.1, s32[16,24,128]{2,1,0:T(8,128)} %pad_add_fusion.ids_ref), custom_call_target="tpu_custom_call" | custom-call | tf_op jit(solution)/shard_map/pallas_call | solution.py:78
  46.8 0.0 copy-start
  46.8 1.6 %copy-done = bf16[16,16,32,128]{3,2,1,0:T(8,128)(2,1)S(1)} copy-done((bf16[16,16,32,128]{3,2,1,0:T(8,128)(2,1)S(1)}, bf16[16,16,32,128]{3,2,1,0:T(8,128)(2,1)}, u32[]{:S(2)}) %copy-start) | copy-done | bytes 2097176
  48.4 0.0 copy-start.2
  48.4 0.9 copy-done.2
  49.4 0.0 copy-start.3
  49.4 0.7 copy-done.3
  50.0 14.3 %shard_map.56.owned_ref = f32[16,16,16]{2,1,0:T(8,128)S(1)} custom-call(s32[16,24,128]{2,1,0:T(8,128)S(1)} %copy-done.2, s32[256]{0:T(256)S(1)} %copy-done.3, bf16[16,16,32,128]{3,2,1,0:T(8,128)(2,1)S(1)} %copy-done, bf16[256,64,128]{2,1,0:T(8,128)(2,1)} %passages_ref.1), custom_call_target="tpu_custom_call" | custom-call | tf_op jit(solution)/shard_map/pallas_call | solution.py:211
  64.3 0.0 copy-start.1
  64.3 0.6 copy-done.1
  65.0 48.9 %shard_map.57 = f32[16,16,16]{2,1,0:T(8,128)} custom-call(f32[16,16,16]{2,1,0:T(8,128)} %copy-done.1), custom_call_target="tpu_custom_call" | custom-call | tf_op jit(solution)/shard_map/pallas_call | solution.py:124
  113.9 0.0 copy-done.4
  113.9 0.1 copy.7
  114.0 1.9 %select_reduce_fusion = f32[16,8,16]{2,1,0:T(8,128)} fusion(f32[16,16,16]{2,1,0:T(8,128)} %shard_map.57, pred[16,16,8]{2,1,0:T(8,128)(4,1)S(1)} %copy.7), kind=kLoop, calls=%fused_computation | loop fusion | flops 63488 | bytes 26624 | tf_op jit(solution)/shard_map/reduce_sum | solution.py:243
  (4 shorter events, 0.0 us)
Async XLA Ops:
  0.0 113.9 %copy-start.4 = (s32[16,8]{0,1:T(8,128)S(1)}, s32[16,8]{0,1:T(8,128)}, u32[]{:S(2)}) copy-start(s32[16,8]{0,1:T(8,128)} %param.8) | copy-start | bytes 1540
  46.8 1.6 %copy-start = (bf16[16,16,32,128]{3,2,1,0:T(8,128)(2,1)S(1)}, bf16[16,16,32,128]{3,2,1,0:T(8,128)(2,1)}, u32[]{:S(2)}) copy-start(bf16[16,16,32,128]{3,2,1,0:T(8,128)(2,1)} %get-tuple-element.8.q_ref) | copy-start | bytes 6291460
  48.4 0.9 copy-start.2
  49.4 0.7 copy-start.3
  64.3 0.7 copy-start.1

commit v2 on v1

--- a/solution.py
+++ b/solution.py
@@ -26,64 +26,101 @@
     return lax.axis_index("shard") * lax.axis_size("sub") + lax.axis_index("sub")
 
 
-def gather_kernel(q_ref, ids_ref, all_q, all_ids, own_sem, q_send, q_recv, ids_send, ids_recv):
-    count = ids_ref.shape[0]
-    me = position()
-    local_q = pltpu.make_async_copy(q_ref, all_q.at[me], own_sem.at[0])
-    local_ids = pltpu.make_async_copy(ids_ref.at[me], all_ids.at[me], own_sem.at[1])
-    local_q.start()
-    local_ids.start()
-    greet(me, count)
-
-    def copies(off):
-        peer = lax.rem(me + off, count)
-        ids = pltpu.make_async_remote_copy(
-            src_ref=ids_ref.at[peer],
-            dst_ref=all_ids.at[me],
-            send_sem=ids_send.at[off],
-            recv_sem=ids_recv.at[off],
-            device_id=place(peer),
-            device_id_type=pl.DeviceIdType.MESH,
-        )
-        tok = pltpu.make_async_remote_copy(
-            src_ref=q_ref,
-            dst_ref=all_q.at[me],
-            send_sem=q_send.at[off],
-            recv_sem=q_recv.at[off],
-            device_id=place(peer),
-            device_id_type=pl.DeviceIdType.MESH,
-        )
-        return ids, tok
-
-    def start(off, carry):
-        ids, tok = copies(off)
-        ids.start()
-        tok.start()
-        return carry
-
-    def finish(off, carry):
-        ids, tok = copies(off)
-        ids.wait()
-        tok.wait()
-        return carry
-
-    lax.fori_loop(1, count, start, 0)
-    lax.fori_loop(1, count, finish, 0)
-    local_q.wait()
-    local_ids.wait()
+def gather_kernel(q_ref, ids_ref, all_q, all_ids, own_sem, z_send, z_recv, x_send, x_recv, c_send, c_recv):
+    depth = lax.axis_size("shard")
+    subs = lax.axis_size("sub")
+    width = subs // 2
+    z, s = lax.axis_index("shard"), lax.axis_index("sub")
+    x, core = s // 2, lax.rem(s, 2)
+    pairs = ((q_ref, all_q), (ids_ref, all_ids))
+
+    def row(block_z, block_x, block_core):
+        return block_z * subs + block_x * 2 + block_core
+
+    def along(step, size, at):
+        return lax.rem(at + size + step, size)
+
+    across = {"shard": z, "sub": x * 2 + 1 - core}
+    z_peers = [{"shard": along(dz, depth, z), "sub": s} for dz in range(depth)]
+    x_peers = [{"shard": z, "sub": along(dx, width, x) * 2 + core} for dx in range(width)]
+    mesh_ids = pl.DeviceIdType.MESH
+
+    local = [pltpu.make_async_copy(own, every.at[row(z, x, core)], own_sem.at[i]) for i, (own, every) in enumerate(pairs)]
+    for copy in local:
+        copy.start()
+    barrier = pltpu.get_barrier_semaphore()
+    for peer in z_peers[1:] + x_peers[1:] + [across]:
+        pl.semaphore_signal(barrier, inc=1, device_id=peer, device_id_type=mesh_ids)
+    pl.semaphore_wait(barrier, depth + width - 1)
+
+    def send(block, own, peer, send_sem, recv_sem):
+        copies = [
+            pltpu.make_async_remote_copy(
+                src_ref=mine if own else every.at[block],
+                dst_ref=every.at[block],
+                send_sem=send_sem(i),
+                recv_sem=recv_sem(i),
+                device_id=peer,
+                device_id_type=mesh_ids,
+            )
+            for i, (mine, every) in enumerate(pairs)
+        ]
+        for copy in copies:
+            copy.start()
+        return copies
+
+    by_z, by_x, by_core = {}, {}, []
+    for dz in range(1, depth):
+        by_z[dz] = send(
+            row(z, x, core), True, z_peers[dz], lambda i: z_send.at[i, dz], lambda i: z_recv.at[i, dz]
+        )
+
+    def pass_on(dz):
+        block = row(along(-dz, depth, z), x, core)
+        for dx in range(1, width):
+            by_x[dz, dx] = send(
+                block, dz == 0, x_peers[dx], lambda i: x_send.at[i, dz, dx], lambda i: x_recv.at[i, dz, dx]
+            )
+        by_core.extend(send(block, dz == 0, across, lambda i: c_send.at[i, dz, 0], lambda i: c_recv.at[i, dz, 0]))
+
+    def cross(dz):
+        for dx in range(1, width):
+            for copy in by_x[dz, dx]:
+                copy.wait_recv()
+            block = row(along(-dz, depth, z), along(-dx, width, x), core)
+            by_core.extend(
+                send(block, False, across, lambda i: c_send.at[i, dz, dx], lambda i: c_recv.at[i, dz, dx])
+            )
+
+    pass_on(0)
+    for dz in range(1, depth):
+        for copy in by_z[dz]:
+            copy.wait_recv()
+        pass_on(dz)
+    for dz in range(depth):
+        cross(dz)
+    for copy in by_core:
+        copy.wait()
+    for copies in list(by_z.values()) + list(by_x.values()):
+        for copy in copies:
+            copy.wait_send()
+    for copy in local:
+        copy.wait()
 
 
 def gather(queries, ids):
-    count = ids.shape[0]
+    depth, subs = lax.axis_size("shard"), lax.axis_size("sub")
+    count = depth * subs
+    sem = pltpu.SemaphoreType.DMA
     return pl.pallas_call(
         gather_kernel,
         out_shape=(
             jax.ShapeDtypeStruct((count,) + queries.shape, queries.dtype),
-            jax.ShapeDtypeStruct(ids.shape, ids.dtype),
+            jax.ShapeDtypeStruct((count,) + ids.shape, ids.dtype),
         ),
         in_specs=[pl.BlockSpec(memory_space=pl.ANY)] * 2,
         out_specs=[pl.BlockSpec(memory_space=pl.ANY)] * 2,
-        scratch_shapes=[pltpu.SemaphoreType.DMA((2,))] + [pltpu.SemaphoreType.DMA((count,))] * 4,
+        scratch_shapes=[sem((2,))] + [sem((2, depth))] * 2 + [sem((2, depth, subs // 2))] * 4,
         compiler_params=pltpu.CompilerParams(collective_id=0, has_side_effects=True),
     )(queries, ids)
 
@@ -131,7 +168,7 @@
     )(owned)
 
 
-def score_kernel(ids_ref, len_ref, q_ref, passages_ref, out_ref, maxima, filled, live):
+def score_kernel(ids_ref, len_ref, q_ref, passages_ref, out_ref, maxima, filled, live, route):
     sources, per_source, query_len, feature = q_ref.shape
     slots = sources * per_source
     passage_count, tokens, _ = passages_ref.shape
@@ -151,20 +188,25 @@
 
         lax.fori_loop(0, passage_count, fill, 0, unroll=8)
 
-    count = jnp.int32(0)
-    for query in range(per_source):
-
-        def collect(source, count, query=query):
-            live[count] = source * per_source + query
-            return count + (ids_ref[source, per_source, query] >= 0).astype(jnp.int32)
-
-        count = lax.fori_loop(0, sources, collect, count, unroll=True)
+    me = position()
+    routes = ids_ref.shape[2] // per_source
+
+    def collect(slot, count):
+        source, query = slot // per_source, lax.rem(slot, per_source)
+        found = jnp.int32(-1)
+        for r in range(routes):
+            found = jnp.where(ids_ref[source, per_source, query * routes + r] == me, r, found)
+        route[slot] = found
+        live[count] = slot
+        return count + (found >= 0).astype(jnp.int32)
+
+    count = lax.fori_loop(0, slots, collect, jnp.int32(0), unroll=4)
     live[count] = live[jnp.maximum(count - 1, 0)]
     blank = jnp.zeros((query_len, feature), jnp.bfloat16)
 
     def one(slot):
         source, query = slot // per_source, lax.rem(slot, per_source)
-        base = ids_ref[source, per_source, query] * cand_count
+        base = route[slot] * cand_count
         tok = q_ref[source, query]
         weights = jnp.concatenate(
             [jnp.concatenate([tok, blank], 1), jnp.concatenate([blank, tok], 1)], 0
@@ -223,6 +265,7 @@
             pltpu.VMEM((cand_count // 2, slots, 2 * query_len), jnp.float32),
             pltpu.VMEM(passages.shape, passages.dtype),
             pltpu.SMEM((slots + 1,), jnp.int32),
+            pltpu.SMEM((slots,), jnp.int32),
         ],
         compiler_params=pltpu.CompilerParams(vmem_limit_bytes=48 << 20),
     )(ids, pass_len, queries, passages)
@@ -232,14 +275,11 @@
     owner_count = lax.axis_size("shard") * lax.axis_size("sub")
     query_count, route_count, cand_count = candidates.shape
     flat = candidates.reshape(query_count, route_count * cand_count)
-    owner_ids = jnp.arange(owner_count, dtype=jnp.int32)
-    numbers = jnp.arange(1, route_count + 1, dtype=jnp.int32)
-    hit = owners[None, :, :] == owner_ids[:, None, None]
-    route = jnp.sum(jnp.where(hit, numbers, 0), axis=2) - 1
-    route = jnp.pad(route[:, None, :], ((0, 0), (0, 7), (0, flat.shape[1] - query_count)))
-    ids = jnp.concatenate([jnp.broadcast_to(flat[None], (owner_count,) + flat.shape), route], axis=1)
+    spare = jnp.zeros((7, flat.shape[1]), jnp.int32)
+    ids = jnp.concatenate([flat, owners.reshape(1, query_count * route_count), spare], axis=0)
     all_q, all_ids = gather(queries, ids)
     returned = give_back(score_slots(all_ids, pass_len, all_q, passages, cand_count))
+    hit = owners[None, :, :] == jnp.arange(owner_count, dtype=jnp.int32)[:, None, None]
     return jnp.sum(jnp.where(hit[..., None], returned[:, :, None, :], 0.0), axis=0)
 
 

time: 115 us -> 94.8 us (0.82)
  Pallas kernels: 108 us -> 87.2 us
    pallas_call x1, Pallas kernels: 48.9 us -> 27.6 us  [give_back(): pl.pallas_call(return_kernel, out_shape=jax.ShapeDtypeStruct(owned.shape,...]
    pallas_call x1, Pallas kernels: 14.3 us -> 33.5 us  [score_slots(): pl.pallas_call(score_kernel, grid=(count // sources,), out_shape=jax.Shap...]
    pallas_call x1, Pallas kernels: 44.3 us -> 26.2 us  [gather(): pl.pallas_call(gather_kernel, out_shape=(jax.ShapeDtypeStruct((count,) +...]
    unnamed x10 -> x9, local copies, waits for them, and re-layouts: 3.84 us -> 4.59 us
where the time goes in v2:
time: 94.8 us; the launch traced here: 95.5 us
  Pallas kernels  87.2 us (92%)
  local copies, waits for them, and re-layouts  5.67 us (6%)
  other arithmetic  2.57 us (3%)
    pallas_call x1, Pallas kernels, score_slots(): pl.pallas_call(score_kernel, grid=(count // sources,), out_shape=jax.Shap...  33.5 us
    pallas_call x1, Pallas kernels, give_back(): pl.pallas_call(return_kernel, out_shape=jax.ShapeDtypeStruct(owned.shape,...  27.6 us
    pallas_call x1, Pallas kernels, gather(): pl.pallas_call(gather_kernel, out_shape=(jax.ShapeDtypeStruct((count,) +...  26.2 us
    unnamed x9, local copies, waits for them, and re-layouts  4.59 us

profile of v2, /device:TPU:0, one launch (start us, length us, event | category | flops | bytes accessed | tf_op | source)
XLA Modules:
  0.0 95.5 jit_solution(11547251598454817735)
XLA Ops:
  0.0 0.8 copy.10
  0.8 0.1 reshape.12
  0.8 0.9 reshape.11
  1.8 0.1 pad.2.clone
  1.9 0.7 add_add_fusion.ids_ref
  2.5 26.2 %shard_map.55 = (bf16[16,16,32,128]{3,2,1,0:T(8,128)(2,1)}, s32[16,24,128]{2,1,0:T(8,128)}) custom-call(bf16[16,32,128]{2,1,0:T(8,128)(2,1)} %q_ref.1, s32[24,128]{1,0:T(8,128)} %add_add_fusion.ids_ref), custom_call_target="tpu_custom_call" | custom-call | tf_op jit(solution)/shard_map/pallas_call | solution.py:115
  28.7 0.0 copy-start
  28.7 1.6 %copy-done = bf16[16,16,32,128]{3,2,1,0:T(8,128)(2,1)S(1)} copy-done((bf16[16,16,32,128]{3,2,1,0:T(8,128)(2,1)S(1)}, bf16[16,16,32,128]{3,2,1,0:T(8,128)(2,1)}, u32[]{:S(2)}) %copy-start) | copy-done | bytes 2097176
  30.3 0.0 copy-start.2
  30.3 0.9 copy-done.2
  31.2 0.0 copy-start.3
  31.2 0.7 copy-done.3
  31.9 33.5 %shard_map.56.owned_ref = f32[16,16,16]{2,1,0:T(8,128)S(1)} custom-call(s32[16,24,128]{2,1,0:T(8,128)S(1)} %copy-done.2, s32[256]{0:T(256)S(1)} %copy-done.3, bf16[16,16,32,128]{3,2,1,0:T(8,128)(2,1)S(1)} %copy-done, bf16[256,64,128]{2,1,0:T(8,128)(2,1)} %passages_ref.1), custom_call_target="tpu_custom_call" | custom-call | tf_op jit(solution)/shard_map/pallas_call | solution.py:253
  65.4 0.0 copy-start.1
  65.4 0.6 copy-done.1
  66.0 27.6 %shard_map.57 = f32[16,16,16]{2,1,0:T(8,128)} custom-call(f32[16,16,16]{2,1,0:T(8,128)} %copy-done.1), custom_call_target="tpu_custom_call" | custom-call | tf_op jit(solution)/shard_map/pallas_call | solution.py:161
  93.7 1.9 %select_reduce_fusion = f32[16,8,16]{2,1,0:T(8,128)} fusion(f32[16,16,16]{2,1,0:T(8,128)} %shard_map.57, pred[16,16,8]{2,1,0:T(8,128)(4,1)S(1)} %iota_compare_fusion), kind=kLoop, calls=%fused_computation | loop fusion | flops 63488 | bytes 26624 | tf_op jit(solution)/shard_map/reduce_sum | solution.py:283
  (2 shorter events, 0.0 us)
Async XLA Ops:
  28.7 1.6 %copy-start = (bf16[16,16,32,128]{3,2,1,0:T(8,128)(2,1)S(1)}, bf16[16,16,32,128]{3,2,1,0:T(8,128)(2,1)}, u32[]{:S(2)}) copy-start(bf16[16,16,32,128]{3,2,1,0:T(8,128)(2,1)} %get-tuple-element.8.q_ref) | copy-start | bytes 6291460
  30.3 0.9 copy-start.2
  31.2 0.7 copy-start.3
  65.4 0.6 copy-start.1

commit v3 on v2

--- a/solution.py
+++ b/solution.py
@@ -168,7 +168,7 @@
     )(owned)
 
 
-def score_kernel(ids_ref, len_ref, q_ref, passages_ref, out_ref, maxima, filled, live, route):
+def score_kernel(route_ref, ids_ref, len_ref, q_ref, passages_ref, out_ref, maxima, filled, live):
     sources, per_source, query_len, feature = q_ref.shape
     slots = sources * per_source
     passage_count, tokens, _ = passages_ref.shape
@@ -188,25 +188,17 @@
 
         lax.fori_loop(0, passage_count, fill, 0, unroll=8)
 
-    me = position()
-    routes = ids_ref.shape[2] // per_source
-
     def collect(slot, count):
-        source, query = slot // per_source, lax.rem(slot, per_source)
-        found = jnp.int32(-1)
-        for r in range(routes):
-            found = jnp.where(ids_ref[source, per_source, query * routes + r] == me, r, found)
-        route[slot] = found
         live[count] = slot
-        return count + (found >= 0).astype(jnp.int32)
-
-    count = lax.fori_loop(0, slots, collect, jnp.int32(0), unroll=4)
+        return count + (route_ref[slot // per_source, lax.rem(slot, per_source)] >= 0).astype(jnp.int32)
+
+    count = lax.fori_loop(0, slots, collect, jnp.int32(0), unroll=16)
     live[count] = live[jnp.maximum(count - 1, 0)]
     blank = jnp.zeros((query_len, feature), jnp.bfloat16)
 
     def one(slot):
         source, query = slot // per_source, lax.rem(slot, per_source)
-        base = route[slot] * cand_count
+        base = route_ref[source, query] * cand_count
         tok = q_ref[source, query]
         weights = jnp.concatenate(
             [jnp.concatenate([tok, blank], 1), jnp.concatenate([blank, tok], 1)], 0
@@ -246,7 +238,7 @@
     out_ref[...] = (total * (1.0 / query_len)).reshape(out_ref.shape)
 
 
-def score_slots(ids, pass_len, queries, passages, cand_count):
+def score_slots(route, ids, pass_len, queries, passages, cand_count):
     count, per_source, query_len, feature = queries.shape
     sources = min(count, 16)
     slots = sources * per_source
@@ -255,6 +247,7 @@
         grid=(count // sources,),
         out_shape=jax.ShapeDtypeStruct((count, per_source, cand_count), jnp.float32),
         in_specs=[
+            pl.BlockSpec((sources, per_source), lambda i: (i, 0), memory_space=pltpu.SMEM),
             pl.BlockSpec((sources,) + ids.shape[1:], lambda i: (i, 0, 0), memory_space=pltpu.SMEM),
             pl.BlockSpec(memory_space=pltpu.SMEM),
             pl.BlockSpec((sources, per_source, query_len, feature), lambda i: (i, 0, 0, 0)),
@@ -265,10 +258,9 @@
             pltpu.VMEM((cand_count // 2, slots, 2 * query_len), jnp.float32),
             pltpu.VMEM(passages.shape, passages.dtype),
             pltpu.SMEM((slots + 1,), jnp.int32),
-            pltpu.SMEM((slots,), jnp.int32),
         ],
         compiler_params=pltpu.CompilerParams(vmem_limit_bytes=48 << 20),
-    )(ids, pass_len, queries, passages)
+    )(route, ids, pass_len, queries, passages)
 
 
 def body(queries, passages, pass_len, owners, candidates):
@@ -278,7 +270,14 @@
     spare = jnp.zeros((7, flat.shape[1]), jnp.int32)
     ids = jnp.concatenate([flat, owners.reshape(1, query_count * route_count), spare], axis=0)
     all_q, all_ids = gather(queries, ids)
-    returned = give_back(score_slots(all_ids, pass_len, all_q, passages, cand_count))
+    place_in_row = jnp.arange(query_count * route_count, dtype=jnp.int32)
+    number = (lax.rem(place_in_row, route_count) + 1).astype(jnp.float32)
+    named = jnp.where(all_ids[:, query_count, :] == position(), number[None, :], 0.0)
+    fold = place_in_row[:, None] // route_count == jnp.arange(query_count, dtype=jnp.int32)[None, :]
+    route = jnp.dot(
+        named.astype(jnp.bfloat16), fold.astype(jnp.bfloat16), preferred_element_type=jnp.float32
+    ).astype(jnp.int32) - 1
+    returned = give_back(score_slots(route, all_ids, pass_len, all_q, passages, cand_count))
     hit = owners[None, :, :] == jnp.arange(owner_count, dtype=jnp.int32)[:, None, None]
     return jnp.sum(jnp.where(hit[..., None], returned[:, :, None, :], 0.0), axis=0)
 

time: 94.8 us -> 89.5 us (0.944); the launches traced: 95.5 us -> 88.6 us
  Pallas kernels: 87.2 us -> 79.3 us
    pallas_call x1, Pallas kernels: 27.6 us -> 7.15 us  [give_back(): pl.pallas_call(return_kernel, out_shape=jax.ShapeDtypeStruct(owned.shape,...]
    pallas_call x1, Pallas kernels: 33.5 us -> 45.9 us  [score_slots(): pl.pallas_call(score_kernel, grid=(count // sources,), out_shape=jax.Shap...]
where the time goes in v3:
time: 89.5 us; the launch traced here: 88.6 us
  Pallas kernels  79.3 us (89%)
  local copies, waits for them, and re-layouts  5.68 us (6%)
  other arithmetic  3.43 us (4%)
    pallas_call x1, Pallas kernels, score_slots(): pl.pallas_call(score_kernel, grid=(count // sources,), out_shape=jax.Shap...  45.9 us
    pallas_call x1, Pallas kernels, gather(): pl.pallas_call(gather_kernel, out_shape=(jax.ShapeDtypeStruct((count,) +...  26.2 us
    pallas_call x1, Pallas kernels, give_back(): pl.pallas_call(return_kernel, out_shape=jax.ShapeDtypeStruct(owned.shape,...  7.15 us
    unnamed x9, local copies, waits for them, and re-layouts  4.6 us
    reduce_sum x1, other arithmetic, body(): jnp.sum(jnp.where(hit[..., None], returned[:, :, None, :], 0.0), axis=0)  1.88 us

profile of v3, /device:TPU:0, one launch (start us, length us, event | category | flops | bytes accessed | tf_op | source)
XLA Modules:
  0.0 88.6 jit_solution(10550362239856422566)
XLA Ops:
  0.0 0.8 copy.10
  0.8 0.1 reshape.57
  0.8 0.9 %reshape.56 = s32[16,128]{1,0:T(8,128)S(1)} reshape(s32[16,8,16]{2,1,0:T(8,128)} %param.9) | data formatting | bytes 16384 | tf_op jit(solution)/shard_map/reshape | solution.py:269
  1.8 0.1 pad.2.clone
  1.9 0.7 add_add_fusion.ids_ref
  2.5 26.2 %shard_map.55 = (bf16[16,16,32,128]{3,2,1,0:T(8,128)(2,1)}, s32[16,24,128]{2,1,0:T(8,128)}) custom-call(bf16[16,32,128]{2,1,0:T(8,128)(2,1)} %q_ref.1, s32[24,128]{1,0:T(8,128)} %add_add_fusion.ids_ref), custom_call_target="tpu_custom_call" | custom-call | tf_op jit(solution)/shard_map/pallas_call | solution.py:115
  28.7 0.9 slice_compare_fusion
  29.6 0.2 fusion.route_ref
  29.8 0.0 copy-start
  29.8 1.6 %copy-done = bf16[16,16,32,128]{3,2,1,0:T(8,128)(2,1)S(1)} copy-done((bf16[16,16,32,128]{3,2,1,0:T(8,128)(2,1)S(1)}, bf16[16,16,32,128]{3,2,1,0:T(8,128)(2,1)}, u32[]{:S(2)}) %copy-start) | copy-done | bytes 2097176
  31.4 0.0 copy-start.2
  31.4 0.9 %copy-done.2 = s32[16,24,128]{2,1,0:T(8,128)S(1)} copy-done((s32[16,24,128]{2,1,0:T(8,128)S(1)}, s32[16,24,128]{2,1,0:T(8,128)}, u32[]{:S(2)}) %copy-start.2) | copy-done | bytes 196632
  32.3 0.0 copy-start.3
  32.3 0.7 copy-done.3
  33.0 45.9 %shard_map.56.owned_ref = f32[16,16,16]{2,1,0:T(8,128)S(1)} custom-call(s32[16,16]{1,0:T(8,128)S(1)} %fusion.route_ref, s32[16,24,128]{2,1,0:T(8,128)S(1)} %copy-done.2, s32[256]{0:T(256)S(1)} %copy-done.3, bf16[16,16,32,128]{3,2,1,0:T(8,128)(2,1)S(1)} %copy-done, bf16[256,64,128]{2,1,0:T(8,128)(2,1)} %passages_ref.1), custom_call_target="tpu_custom_call" | custom-call | tf_op jit(solution)/shard_map/pallas_call | solution.py:245
  78.9 0.0 copy-start.1
  78.9 0.6 copy-done.1
  79.6 7.2 %shard_map.57 = f32[16,16,16]{2,1,0:T(8,128)} custom-call(f32[16,16,16]{2,1,0:T(8,128)} %copy-done.1), custom_call_target="tpu_custom_call" | custom-call | tf_op jit(solution)/shard_map/pallas_call | solution.py:161
  86.8 1.9 %select_reduce_fusion = f32[16,8,16]{2,1,0:T(8,128)} fusion(f32[16,16,16]{2,1,0:T(8,128)} %shard_map.57, pred[16,16,8]{2,1,0:T(8,128)(4,1)S(1)} %iota_compare_fusion), kind=kLoop, calls=%fused_computation.2 | loop fusion | flops 63488 | bytes 26624 | tf_op jit(solution)/shard_map/reduce_sum | solution.py:282
  (3 shorter events, 0.0 us)
Async XLA Ops:
  29.8 1.6 %copy-start = (bf16[16,16,32,128]{3,2,1,0:T(8,128)(2,1)S(1)}, bf16[16,16,32,128]{3,2,1,0:T(8,128)(2,1)}, u32[]{:S(2)}) copy-start(bf16[16,16,32,128]{3,2,1,0:T(8,128)(2,1)} %get-tuple-element.8.q_ref) | copy-start | bytes 6291460
  31.4 0.9 %copy-start.2 = (s32[16,24,128]{2,1,0:T(8,128)S(1)}, s32[16,24,128]{2,1,0:T(8,128)}, u32[]{:S(2)}) copy-start(s32[16,24,128]{2,1,0:T(8,128)} %get-tuple-element.7.ids_ref) | copy-start | bytes 589828
  32.3 0.7 copy-start.3
  78.9 0.6 copy-start.1

commit v4 on v3

--- a/solution.py
+++ b/solution.py
@@ -193,7 +193,8 @@
         return count + (route_ref[slot // per_source, lax.rem(slot, per_source)] >= 0).astype(jnp.int32)
 
     count = lax.fori_loop(0, slots, collect, jnp.int32(0), unroll=16)
-    live[count] = live[jnp.maximum(count - 1, 0)]
+    for spare in range(3):
+        live[count + spare] = live[jnp.maximum(count - 1, 0)]
     blank = jnp.zeros((query_len, feature), jnp.bfloat16)
 
     def one(slot):
@@ -216,12 +217,12 @@
             best = jnp.max(similar[g * tokens : (g + 1) * tokens], axis=0, keepdims=True)
             maxima[g, pl.ds(slot, 1), :] = best
 
-    def pair(step, carry):
-        one(live[2 * step])
-        one(live[2 * step + 1])
-        return carry
-
-    lax.fori_loop(0, (count + 1) // 2, pair, 0)
+    def several(step, carry):
+        for turn in range(4):
+            one(live[4 * step + turn])
+        return carry
+
+    lax.fori_loop(0, (count + 3) // 4, several, 0)
 
     width = 2 * query_len
     lane = lax.broadcasted_iota(jnp.int32, (width, cand_count), 0)
@@ -257,7 +258,7 @@
         scratch_shapes=[
             pltpu.VMEM((cand_count // 2, slots, 2 * query_len), jnp.float32),
             pltpu.VMEM(passages.shape, passages.dtype),
-            pltpu.SMEM((slots + 1,), jnp.int32),
+            pltpu.SMEM((slots + 3,), jnp.int32),
         ],
         compiler_params=pltpu.CompilerParams(vmem_limit_bytes=48 << 20),
     )(route, ids, pass_len, queries, passages)

time: 89.5 us -> 79.6 us (0.89)
  Pallas kernels: 79.3 us -> 69.2 us
    pallas_call x1, Pallas kernels: 45.9 us -> 17.5 us  [score_slots(): pl.pallas_call(score_kernel, grid=(count // sources,), out_shape=jax.Shap...]
    pallas_call x1, Pallas kernels: 7.15 us -> 25.5 us  [give_back(): pl.pallas_call(return_kernel, out_shape=jax.ShapeDtypeStruct(owned.shape,...]
where the time goes in v4:
time: 79.6 us; the launch traced here: 78.6 us
  Pallas kernels  69.2 us (87%)
  local copies, waits for them, and re-layouts  5.68 us (7%)
  other arithmetic  3.43 us (4%)
    pallas_call x1, Pallas kernels, gather(): pl.pallas_call(gather_kernel, out_shape=(jax.ShapeDtypeStruct((count,) +...  26.2 us
    pallas_call x1, Pallas kernels, give_back(): pl.pallas_call(return_kernel, out_shape=jax.ShapeDtypeStruct(owned.shape,...  25.5 us
    pallas_call x1, Pallas kernels, score_slots(): pl.pallas_call(score_kernel, grid=(count // sources,), out_shape=jax.Shap...  17.5 us
    unnamed x9, local copies, waits for them, and re-layouts  4.6 us
    reduce_sum x1, other arithmetic, body(): jnp.sum(jnp.where(hit[..., None], returned[:, :, None, :], 0.0), axis=0)  1.88 us

profile of v4, /device:TPU:0, one launch (start us, length us, event | category | flops | bytes accessed | tf_op | source)
XLA Modules:
  0.0 78.6 jit_solution(7937836596530796314)
XLA Ops:
  0.0 0.8 copy.10
  0.8 0.1 reshape.57
  0.8 0.9 %reshape.56 = s32[16,128]{1,0:T(8,128)S(1)} reshape(s32[16,8,16]{2,1,0:T(8,128)} %param.9) | data formatting | bytes 16384 | tf_op jit(solution)/shard_map/reshape | solution.py:270
  1.8 0.1 pad.2.clone
  1.9 0.7 add_add_fusion.ids_ref
  2.5 26.2 %shard_map.55 = (bf16[16,16,32,128]{3,2,1,0:T(8,128)(2,1)}, s32[16,24,128]{2,1,0:T(8,128)}) custom-call(bf16[16,32,128]{2,1,0:T(8,128)(2,1)} %q_ref.1, s32[24,128]{1,0:T(8,128)} %add_add_fusion.ids_ref), custom_call_target="tpu_custom_call" | custom-call | tf_op jit(solution)/shard_map/pallas_call | solution.py:115
  28.7 0.9 %slice_compare_fusion = pred[16,1,128]{2,1,0:T(4,128)(4,1)S(1)} fusion(s32[16,24,128]{2,1,0:T(8,128)} %get-tuple-element.7.ids_ref, s32[]{:T(128)S(6)} %add.20), kind=kLoop, calls=%fused_computation.8 | loop fusion | flops 2048 | bytes 10244 | tf_op jit(solution)/shard_map/eq | solution.py:276
  29.6 0.2 fusion.route_ref
  29.8 0.0 copy-start
  29.8 1.6 %copy-done = bf16[16,16,32,128]{3,2,1,0:T(8,128)(2,1)S(1)} copy-done((bf16[16,16,32,128]{3,2,1,0:T(8,128)(2,1)S(1)}, bf16[16,16,32,128]{3,2,1,0:T(8,128)(2,1)}, u32[]{:S(2)}) %copy-start) | copy-done | bytes 2097176
  31.4 0.0 copy-start.2
  31.4 0.9 %copy-done.2 = s32[16,24,128]{2,1,0:T(8,128)S(1)} copy-done((s32[16,24,128]{2,1,0:T(8,128)S(1)}, s32[16,24,128]{2,1,0:T(8,128)}, u32[]{:S(2)}) %copy-start.2) | copy-done | bytes 196632
  32.3 0.0 copy-start.3
  32.3 0.7 copy-done.3
  33.0 17.5 %shard_map.56.owned_ref = f32[16,16,16]{2,1,0:T(8,128)S(1)} custom-call(s32[16,16]{1,0:T(8,128)S(1)} %fusion.route_ref, s32[16,24,128]{2,1,0:T(8,128)S(1)} %copy-done.2, s32[256]{0:T(256)S(1)} %copy-done.3, bf16[16,16,32,128]{3,2,1,0:T(8,128)(2,1)S(1)} %copy-done, bf16[256,64,128]{2,1,0:T(8,128)(2,1)} %passages_ref.1), custom_call_target="tpu_custom_call" | custom-call | tf_op jit(solution)/shard_map/pallas_call | solution.py:246
  50.5 0.0 copy-start.1
  50.5 0.6 copy-done.1
  51.2 25.5 %shard_map.57 = f32[16,16,16]{2,1,0:T(8,128)} custom-call(f32[16,16,16]{2,1,0:T(8,128)} %copy-done.1), custom_call_target="tpu_custom_call" | custom-call | tf_op jit(solution)/shard_map/pallas_call | solution.py:161
  76.7 1.9 %select_reduce_fusion = f32[16,8,16]{2,1,0:T(8,128)} fusion(f32[16,16,16]{2,1,0:T(8,128)} %shard_map.57, pred[16,16,8]{2,1,0:T(8,128)(4,1)S(1)} %iota_compare_fusion), kind=kLoop, calls=%fused_computation.2 | loop fusion | flops 63488 | bytes 26624 | tf_op jit(solution)/shard_map/reduce_sum | solution.py:283
  (3 shorter events, 0.0 us)
Async XLA Ops:
  29.8 1.6 %copy-start = (bf16[16,16,32,128]{3,2,1,0:T(8,128)(2,1)S(1)}, bf16[16,16,32,128]{3,2,1,0:T(8,128)(2,1)}, u32[]{:S(2)}) copy-start(bf16[16,16,32,128]{3,2,1,0:T(8,128)(2,1)} %get-tuple-element.8.q_ref) | copy-start | bytes 6291460
  31.4 0.9 %copy-start.2 = (s32[16,24,128]{2,1,0:T(8,128)S(1)}, s32[16,24,128]{2,1,0:T(8,128)}, u32[]{:S(2)}) copy-start(s32[16,24,128]{2,1,0:T(8,128)} %get-tuple-element.7.ids_ref) | copy-start | bytes 589828
  32.3 0.7 copy-start.3
  50.5 0.6 copy-start.1

commit v5 on v4

--- a/solution.py
+++ b/solution.py
@@ -193,7 +193,7 @@
         return count + (route_ref[slot // per_source, lax.rem(slot, per_source)] >= 0).astype(jnp.int32)
 
     count = lax.fori_loop(0, slots, collect, jnp.int32(0), unroll=16)
-    for spare in range(3):
+    for spare in range(7):
         live[count + spare] = live[jnp.maximum(count - 1, 0)]
     blank = jnp.zeros((query_len, feature), jnp.bfloat16)
 
@@ -218,11 +218,11 @@
             maxima[g, pl.ds(slot, 1), :] = best
 
     def several(step, carry):
-        for turn in range(4):
-            one(live[4 * step + turn])
-        return carry
-
-    lax.fori_loop(0, (count + 3) // 4, several, 0)
+        for turn in range(8):
+            one(live[8 * step + turn])
+        return carry
+
+    lax.fori_loop(0, (count + 7) // 8, several, 0)
 
     width = 2 * query_len
     lane = lax.broadcasted_iota(jnp.int32, (width, cand_count), 0)
@@ -258,7 +258,7 @@
         scratch_shapes=[
             pltpu.VMEM((cand_count // 2, slots, 2 * query_len), jnp.float32),
             pltpu.VMEM(passages.shape, passages.dtype),
-            pltpu.SMEM((slots + 3,), jnp.int32),
+            pltpu.SMEM((slots + 7,), jnp.int32),
         ],
         compiler_params=pltpu.CompilerParams(vmem_limit_bytes=48 << 20),
     )(route, ids, pass_len, queries, passages)

time: 79.6 us -> 73.7 us (0.926); the launches traced: 78.6 us -> 74.2 us
  Pallas kernels: 69.2 us -> 64.8 us
    pallas_call x1, Pallas kernels: 17.5 us -> 13.6 us  [score_slots(): pl.pallas_call(score_kernel, grid=(count // sources,), out_shape=jax.Shap...]
where the time goes in v5:
time: 73.7 us; the launch traced here: 74.2 us
  Pallas kernels  64.8 us (88%)
  local copies, waits for them, and re-layouts  5.68 us (8%)
  other arithmetic  3.43 us (5%)
    pallas_call x1, Pallas kernels, gather(): pl.pallas_call(gather_kernel, out_shape=(jax.ShapeDtypeStruct((count,) +...  26.2 us
    pallas_call x1, Pallas kernels, give_back(): pl.pallas_call(return_kernel, out_shape=jax.ShapeDtypeStruct(owned.shape,...  25 us
    pallas_call x1, Pallas kernels, score_slots(): pl.pallas_call(score_kernel, grid=(count // sources,), out_shape=jax.Shap...  13.6 us
    unnamed x9, local copies, waits for them, and re-layouts  4.6 us
    reduce_sum x1, other arithmetic, body(): jnp.sum(jnp.where(hit[..., None], returned[:, :, None, :], 0.0), axis=0)  1.88 us

profile of v5, /device:TPU:0, one launch (start us, length us, event | category | flops | bytes accessed | tf_op | source)
XLA Modules:
  0.0 74.2 jit_solution(7256276245491900290)
XLA Ops:
  0.0 0.8 %copy.10 = s32[16,8]{1,0:T(8,128)S(1)} copy(s32[16,8]{0,1:T(8,128)} %param.8) | data formatting | bytes 1024 | tf_op args[3]
  0.8 0.1 reshape.57
  0.8 0.9 %reshape.56 = s32[16,128]{1,0:T(8,128)S(1)} reshape(s32[16,8,16]{2,1,0:T(8,128)} %param.9) | data formatting | bytes 16384 | tf_op jit(solution)/shard_map/reshape | solution.py:270
  1.8 0.1 pad.2.clone
  1.9 0.7 add_add_fusion.ids_ref
  2.5 26.2 %shard_map.55 = (bf16[16,16,32,128]{3,2,1,0:T(8,128)(2,1)}, s32[16,24,128]{2,1,0:T(8,128)}) custom-call(bf16[16,32,128]{2,1,0:T(8,128)(2,1)} %q_ref.1, s32[24,128]{1,0:T(8,128)} %add_add_fusion.ids_ref), custom_call_target="tpu_custom_call" | custom-call | tf_op jit(solution)/shard_map/pallas_call | solution.py:115
  28.7 0.9 %slice_compare_fusion = pred[16,1,128]{2,1,0:T(4,128)(4,1)S(1)} fusion(s32[16,24,128]{2,1,0:T(8,128)} %get-tuple-element.7.ids_ref, s32[]{:T(128)S(6)} %add.20), kind=kLoop, calls=%fused_computation.8 | loop fusion | flops 2048 | bytes 10244 | tf_op jit(solution)/shard_map/eq | solution.py:276
  29.6 0.2 fusion.route_ref
  29.8 0.0 copy-start
  29.8 1.6 %copy-done = bf16[16,16,32,128]{3,2,1,0:T(8,128)(2,1)S(1)} copy-done((bf16[16,16,32,128]{3,2,1,0:T(8,128)(2,1)S(1)}, bf16[16,16,32,128]{3,2,1,0:T(8,128)(2,1)}, u32[]{:S(2)}) %copy-start) | copy-done | bytes 2097176
  31.4 0.0 copy-start.2
  31.4 0.9 %copy-done.2 = s32[16,24,128]{2,1,0:T(8,128)S(1)} copy-done((s32[16,24,128]{2,1,0:T(8,128)S(1)}, s32[16,24,128]{2,1,0:T(8,128)}, u32[]{:S(2)}) %copy-start.2) | copy-done | bytes 196632
  32.3 0.0 copy-start.3
  32.3 0.7 copy-done.3
  33.0 13.6 %shard_map.56.owned_ref = f32[16,16,16]{2,1,0:T(8,128)S(1)} custom-call(s32[16,16]{1,0:T(8,128)S(1)} %fusion.route_ref, s32[16,24,128]{2,1,0:T(8,128)S(1)} %copy-done.2, s32[256]{0:T(256)S(1)} %copy-done.3, bf16[16,16,32,128]{3,2,1,0:T(8,128)(2,1)S(1)} %copy-done, bf16[256,64,128]{2,1,0:T(8,128)(2,1)} %passages_ref.1), custom_call_target="tpu_custom_call" | custom-call | tf_op jit(solution)/shard_map/pallas_call | solution.py:246
  46.6 0.0 copy-start.1
  46.6 0.6 copy-done.1
  47.2 25.0 %shard_map.57 = f32[16,16,16]{2,1,0:T(8,128)} custom-call(f32[16,16,16]{2,1,0:T(8,128)} %copy-done.1), custom_call_target="tpu_custom_call" | custom-call | tf_op jit(solution)/shard_map/pallas_call | solution.py:161
  72.3 1.9 %select_reduce_fusion = f32[16,8,16]{2,1,0:T(8,128)} fusion(f32[16,16,16]{2,1,0:T(8,128)} %shard_map.57, pred[16,16,8]{2,1,0:T(8,128)(4,1)S(1)} %iota_compare_fusion), kind=kLoop, calls=%fused_computation.2 | loop fusion | flops 63488 | bytes 26624 | tf_op jit(solution)/shard_map/reduce_sum | solution.py:283
  (3 shorter events, 0.0 us)
Async XLA Ops:
  29.8 1.6 %copy-start = (bf16[16,16,32,128]{3,2,1,0:T(8,128)(2,1)S(1)}, bf16[16,16,32,128]{3,2,1,0:T(8,128)(2,1)}, u32[]{:S(2)}) copy-start(bf16[16,16,32,128]{3,2,1,0:T(8,128)(2,1)} %get-tuple-element.8.q_ref) | copy-start | bytes 6291460
  31.4 0.9 %copy-start.2 = (s32[16,24,128]{2,1,0:T(8,128)S(1)}, s32[16,24,128]{2,1,0:T(8,128)}, u32[]{:S(2)}) copy-start(s32[16,24,128]{2,1,0:T(8,128)} %get-tuple-element.7.ids_ref) | copy-start | bytes 589828
  32.3 0.7 copy-start.3
  46.6 0.6 copy-start.1
